TPU v7x, 256 devices: a whole 4x4x8 slice. The times are simulated.
256 devices in a mesh: seq: 64 (over z, y_hi, x), head: 4 (over y_lo, core).
Axes of the slice: x: 4, y: 4 (y_hi: 2, y_lo: 2; y = y_hi * 2 + y_lo), z: 8, core: 2. Of those that a mesh axis runs over, the one named last changes fastest.
Arguments:
- queries: bfloat16 [16384, 4096], P('seq', 'head')
- key_states: bfloat16 [16384, 1024], P('seq', 'head')
- value_states: bfloat16 [16384, 1024], P('seq', 'head'), may hold values from -6 to 6
- query_tangent: bfloat16 [16384, 4096], P('seq', 'head'), may hold values from -6 to 6
- key_tangent: bfloat16 [16384, 1024], P('seq', 'head'), may hold values from -6 to 6
- value_tangent: bfloat16 [16384, 1024], P('seq', 'head'), may hold values from -6 to 6
- segment_ids: int32 [16384], P('seq'), may hold values from 0 to 31, never falling along the last dimension, each value on 1 to 1024 neighbouring positions
- out_weight: bfloat16 [4096, 4096], P('head'), may hold values from -0.5 to 0.5
Outputs:
- layer_out: bfloat16 [16384, 4096], P('seq', 'head')
- layer_tangent: bfloat16 [16384, 4096], P('seq', 'head')
All inputs are finite; a program needn't handle non-finite values.
Results may differ from a plain program's by a relative error of at most 0.015.
The roundings to bfloat16 on the way count: a program that leaves them out, or rounds other values in their place, can miss the bound.
Values may be sent and summed in bfloat16 or wider, within the bound.
A program may use at most 128 MiB of HBM per device.

v0:
```python
import math

import jax
import jax.numpy as jnp
from jax import lax
from jax.sharding import PartitionSpec as P

HEADS = 32
KV_HEADS = 8
HD = 128


negative_fill = -1e30


def passed_along(value, axis, steps):
    count = lax.axis_size(axis)
    leading, last = (max(0, -steps), min(count, count - steps))
    return lax.ppermute(value, axis, [(source, source + steps) for source in range(leading, last)])


def key_view(block):
    return block.reshape(block.shape[0], block.shape[1] // HD, HD)


def score_pair(q_heads, qtan_heads, key_block, ktan_block):
    inverse_root = 1.0 / math.sqrt(HD)
    k_heads = key_view(key_block)
    kt_heads = key_view(ktan_block)
    scores = (
        jnp.einsum("qhgd,khd->qhgk", q_heads, k_heads, preferred_element_type=jnp.float32)
        * inverse_root
    )
    tangent = (
        jnp.einsum("qhgd,khd->qhgk", qtan_heads, k_heads, preferred_element_type=jnp.float32)
        + jnp.einsum("qhgd,khd->qhgk", q_heads, kt_heads, preferred_element_type=jnp.float32)
    ) * inverse_root
    return (scores, tangent)


def accumulate(weights, tangent, value_block, vtan_block):
    v_heads = key_view(value_block)
    vt_heads = key_view(vtan_block)
    product = weights * tangent
    rounded = weights.astype(jnp.bfloat16)
    weighted = product.astype(jnp.bfloat16)
    accum = jnp.einsum("qhgk,khd->qhgd", rounded, v_heads, preferred_element_type=jnp.float32)
    accum_tan = jnp.einsum(
        "qhgk,khd->qhgd", rounded, vt_heads, preferred_element_type=jnp.float32
    ) + jnp.einsum("qhgk,khd->qhgd", weighted, v_heads, preferred_element_type=jnp.float32)
    return (jnp.sum(weights, axis=-1), jnp.sum(product, axis=-1), accum, accum_tan)


def keep_same(carry_in):
    return carry_in


def per_device(
    queries,
    key_states,
    value_states,
    query_tangent,
    key_tangent,
    value_tangent,
    segment_ids,
    out_weight,
):
    row_count = queries.shape[0]
    group_size = HEADS // KV_HEADS
    q_heads = queries.reshape(row_count, -1, group_size, HD)
    qtan_heads = query_tangent.reshape(row_count, -1, group_size, HD)
    kv_local = key_states.shape[1] // HD
    stat_zero = jnp.zeros((row_count, kv_local, group_size), jnp.float32)
    accum_zero = jnp.zeros((row_count, kv_local, group_size, HD), jnp.float32)
    query_pos = lax.axis_index("seq") * row_count + jnp.arange(row_count, dtype=jnp.int32)
    reach = 3 * row_count

    def fold_block(carry, blocks, key_pos):
        key_block, value_block, ktan_block, vtan_block, key_seg = blocks
        diff = query_pos[:, None] - key_pos[None, :]
        allowed = (
            (diff >= 0)
            & (diff < reach)
            & (key_pos[None, :] >= 0)
            & (key_seg[None, :] == segment_ids[:, None])
        )
        allowed = allowed[:, None, None, :]

        def update(current):
            run_max, run_sum, run_tan, run_accum, run_accum_tan = current
            scores, tangent = score_pair(q_heads, qtan_heads, key_block, ktan_block)
            masked = jnp.where(allowed, scores, negative_fill)
            new_max = jnp.maximum(run_max, jnp.max(masked, axis=-1))
            rescale = jnp.exp(run_max - new_max)
            weights = jnp.where(allowed, jnp.exp(masked - new_max[..., None]), 0.0)
            block_sums = accumulate(weights, tangent, value_block, vtan_block)
            return (
                new_max,
                run_sum * rescale + block_sums[0],
                run_tan * rescale + block_sums[1],
                run_accum * rescale[..., None] + block_sums[2],
                run_accum_tan * rescale[..., None] + block_sums[3],
            )

        return lax.cond(jnp.any(allowed), update, keep_same, carry)

    own = (key_states, value_states, key_tangent, value_tangent, segment_ids)
    carry = (stat_zero + negative_fill, stat_zero, stat_zero, accum_zero, accum_zero)
    carry = fold_block(carry, own, query_pos)
    moving = own
    for back in range(1, 4):
        moving = passed_along((moving[0], moving[1], moving[2], moving[3], moving[4]), "seq", 1)
        carry = fold_block(carry, moving, query_pos - back * row_count)
    weight_sum, tangent_sum, accum, accum_tan = (carry[1], carry[2], carry[3], carry[4])
    mixed = accum / weight_sum[..., None]
    mixed_tan = accum_tan / weight_sum[..., None] - (tangent_sum / weight_sum)[..., None] * mixed
    attended_rows = mixed.astype(jnp.bfloat16).reshape(row_count, -1)
    tangent_rows = mixed_tan.astype(jnp.bfloat16).reshape(row_count, -1)
    out_term = jnp.dot(attended_rows, out_weight, preferred_element_type=jnp.float32)
    tan_term = jnp.dot(tangent_rows, out_weight, preferred_element_type=jnp.float32)
    layer_out, layer_tangent = (
        lax.psum_scatter(
            out_term.astype(jnp.bfloat16), "head", scatter_dimension=1, tiled=True
        ).astype(jnp.float32),
        lax.psum_scatter(
            tan_term.astype(jnp.bfloat16), "head", scatter_dimension=1, tiled=True
        ).astype(jnp.float32),
    )
    return (layer_out.astype(jnp.bfloat16), layer_tangent.astype(jnp.bfloat16))


def solution(mesh):
    return jax.shard_map(
        per_device,
        mesh=mesh,
        in_specs=(
            P("seq", "head"),
            P("seq", "head"),
            P("seq", "head"),
            P("seq", "head"),
            P("seq", "head"),
            P("seq", "head"),
            P("seq"),
            P("head", None),
        ),
        out_specs=(P("seq", "head"), P("seq", "head")),
        check_vma=False,
    )
```

profile of v0, /device:TPU:112, one launch (start us, length us, event | category | flops | bytes accessed | tf_op | source)
XLA Modules:
  0.0 240.9 jit_solution(6198553513520064232)
XLA Ops:
  7.2 3.4 %collective-permute-start = (s32[256]{0:T(256)}, s32[256]{0:T(256)S(1)}, u32[]{:S(2)}, u32[]{:S(2)}) collective-permute-start(s32[256]{0:T(256)} %param.22), channel_id=1, source_target_pairs={{0,4},{4,8},{8,12},{12,16},{16,20},{20,24},{24,28},{28,32},{32,36}... | collective-permute-start | bytes 3080 | tf_op jit(solution)/shard_map/ppermute | solution.py:19
  10.6 3.4 %collective-permute-start.3 = (bf16[256,256]{1,0:T(8,128)(2,1)}, bf16[256,256]{1,0:T(8,128)(2,1)S(1)}, u32[]{:S(2)}, u32[]{:S(2)}) collective-permute-start(bf16[256,256]{1,0:T(8,128)(2,1)} %param.17), channel_id=1, source_target_pairs={{0,4},{4,8},{8,12},{12,16},{16,20},{20,24},{24,28},{28,32},{32,36}... | collective-permute-start | bytes 393224 | tf_op jit(solution)/shard_map/ppermute | solution.py:19
  14.0 3.1 %collective-permute-start.4 = (bf16[256,256]{1,0:T(8,128)(2,1)}, bf16[256,256]{1,0:T(8,128)(2,1)S(1)}, u32[]{:S(2)}, u32[]{:S(2)}) collective-permute-start(bf16[256,256]{1,0:T(8,128)(2,1)} %param.20), channel_id=1, source_target_pairs={{0,4},{4,8},{8,12},{12,16},{16,20},{20,24},{24,28},{28,32},{32,36}... | collective-permute-start | bytes 393224 | tf_op jit(solution)/shard_map/ppermute | solution.py:19
  17.2 4.7 %collective-permute-start.5 = (bf16[256,256]{1,0:T(8,128)(2,1)}, bf16[256,256]{1,0:T(8,128)(2,1)S(1)}, u32[]{:S(2)}, u32[]{:S(2)}) collective-permute-start(bf16[256,256]{1,0:T(8,128)(2,1)} %param.18), channel_id=1, source_target_pairs={{0,4},{4,8},{8,12},{12,16},{16,20},{20,24},{24,28},{28,32},{32,36}... | collective-permute-start | bytes 393224 | tf_op jit(solution)/shard_map/ppermute | solution.py:19
  21.9 3.4 %collective-permute-start.6 = (bf16[256,256]{1,0:T(8,128)(2,1)}, bf16[256,256]{1,0:T(8,128)(2,1)S(1)}, u32[]{:S(2)}, u32[]{:S(2)}) collective-permute-start(bf16[256,256]{1,0:T(8,128)(2,1)} %param.21), channel_id=1, source_target_pairs={{0,4},{4,8},{8,12},{12,16},{16,20},{20,24},{24,28},{28,32},{32,36}... | collective-permute-start | bytes 393224 | tf_op jit(solution)/shard_map/ppermute | solution.py:19
  25.3 3.4 %collective-permute-start.1 = (s32[256]{0:T(256)S(1)}, s32[256]{0:T(256)S(1)}, u32[]{:S(2)}, u32[]{:S(2)}) collective-permute-start(s32[256]{0:T(256)S(1)} %collective-permute-done), channel_id=1, source_target_pairs={{0,4},{4,8},{8,12},{12,16},{16,20},{20,24},{24,28},{28,32},{32,36}... | collective-permute-start | bytes 3080 | tf_op jit(solution)/shard_map/ppermute | solution.py:19
  28.7 3.8 %collective-permute-done.6 = bf16[256,256]{1,0:T(8,128)(2,1)S(1)} collective-permute-done((bf16[256,256]{1,0:T(8,128)(2,1)}, bf16[256,256]{1,0:T(8,128)(2,1)S(1)}, u32[]{:S(2)}, u32[]{:S(2)}) %collective-permute-start.6) | collective-permute-done | bytes 131104 | tf_op jit(solution)/shard_map/ppermute | solution.py:19
  32.6 1.9 collective-permute-start.10
  34.5 2.4 collective-permute-start.7
  36.9 3.4 %collective-permute-start.8 = (bf16[256,256]{1,0:T(8,128)(2,1)S(1)}, bf16[256,256]{1,0:T(8,128)(2,1)}, u32[]{:S(2)}, u32[]{:S(2)}) collective-permute-start(bf16[256,256]{1,0:T(8,128)(2,1)S(1)} %collective-permute-done.4), channel_id=1, source_target_pairs={{0,4},{4,8},{8,12},{12,16},{16,20},{20,24},{24,28},{28,32},{32,36}... | collective-permute-start | bytes 393224 | tf_op jit(solution)/shard_map/ppermute | solution.py:19
  40.4 9.3 %collective-permute-start.9 = (bf16[256,256]{1,0:T(8,128)(2,1)S(1)}, bf16[256,256]{1,0:T(8,128)(2,1)}, u32[]{:S(2)}, u32[]{:S(2)}) collective-permute-start(bf16[256,256]{1,0:T(8,128)(2,1)S(1)} %collective-permute-done.5), channel_id=1, source_target_pairs={{0,4},{4,8},{8,12},{12,16},{16,20},{20,24},{24,28},{28,32},{32,36}... | collective-permute-start | bytes 393224 | tf_op jit(solution)/shard_map/ppermute | solution.py:19
  49.7 1.9 collective-permute-start.2
  51.7 1.2 copy.82
  52.9 1.2 copy.83
  54.2 1.9 collective-permute-start.11
  56.1 1.9 collective-permute-start.12
  58.1 4.8 %collective-permute-start.13 = (bf16[256,256]{1,0:T(8,128)(2,1)}, bf16[256,256]{1,0:T(8,128)(2,1)}, u32[]{:S(2)}, u32[]{:S(2)}) collective-permute-start(bf16[256,256]{1,0:T(8,128)(2,1)} %collective-permute-done.9), channel_id=1, source_target_pairs={{0,4},{4,8},{8,12},{12,16},{16,20},{20,24},{24,28},{28,32},{32,36}... | collective-permute-start | bytes 393224 | tf_op jit(solution)/shard_map/ppermute | solution.py:19
  62.9 3.2 %collective-permute-start.14 = (bf16[256,256]{1,0:T(8,128)(2,1)}, bf16[256,256]{1,0:T(8,128)(2,1)}, u32[]{:S(2)}, u32[]{:S(2)}) collective-permute-start(bf16[256,256]{1,0:T(8,128)(2,1)} %collective-permute-done.10), channel_id=1, source_target_pairs={{0,4},{4,8},{8,12},{12,16},{16,20},{20,24},{24,28},{28,32},{32,36}... | collective-permute-start | bytes 393224 | tf_op jit(solution)/shard_map/ppermute | solution.py:19
  66.2 1.4 fusion.86
  70.2 19.1 %conditional.4 = (f32[256,2,4]{0,2,1:T(4,128)}, f32[256,2,4]{0,2,1:T(4,128)S(1)}, f32[256,2,4]{0,2,1:T(4,128)S(1)}, f32[256,2,4,128]{3,0,2,1:T(8,128)S(1)}, f32[256,2,4,128]{3,0,2,1:T(8,128)S(1)}) conditional(s32[]{:T(128)} %convert_element_type.55, () %tuple.35, (pred[256,1,1,256]{0,3,2,1:T(8,128)(4,1)S(1)}, bf16[256,256]{1,0:T(8,128)(2,1)}, ...), branch_computations={%region_4.0_spmd, %region_5.9_spmd} | conditional | flops 820256768 | bytes 35332276 | solution.py:105
  70.2 0.9 reshape.530
  71.1 1.8 fusion
  73.5 1.7 fusion.12
  75.3 3.2 %fusion.98 = (f32[256,2,4]{0,2,1:T(4,128)S(1)}, bf16[256,2,4,256]{0,3,2,1:T(8,128)(2,1)S(1)}) fusion(f32[2,256,256,4]{2,1,3,0:T(8,128)} %fusion.12, bf16[256,2,4,128]{0,3,2,1:T(8,128)(2,1)S(1)} %get-tuple-element.199, bf16[256,2,128,1]{2,1,0,3:T(2,128)(2,1)S(1)} %bitcast.238, f32[256,2,4]{0,2,1:T(4,128)} %get-tuple-element.315, ...), kind=kOutput, calls=%fused_computation.134 | convolution fusion | flops 138934272 | bytes 5980160 | tf_op jit(solution)/shard_map/cond/branch_1_fun/qhgd,khd->qhgk/dot_general | solution.py:36
  78.6 3.4 %fusion.7 = f32[2,256,4,128]{3,1,2,0:T(8,128)} fusion(bf16[256,2,128,1]{2,1,0,3:T(2,128)(2,1)S(1)} %bitcast.242, f32[256,2,4]{0,2,1:T(4,128)} %get-tuple-element.315, f32[2,256,256,4]{2,1,3,0:T(8,128)} %get-tuple-element.263, pred[256,256]{0,1:T(8,128)(4,1)S(1)} %bitcast.213), kind=kOutput, calls=%fused_computation.12 | convolution fusion | flops 136839168 | bytes 3350528 | tf_op jit(solution)/shard_map/cond/branch_1_fun/qhgk,khd->qhgd/dot_general | solution.py:48
  82.7 2.0 fusion.2
  84.6 2.7 %fusion.3 = f32[256,2,4,128]{3,0,2,1:T(8,128)S(1)} fusion(f32[256,2,4]{0,2,1:T(4,128)S(1)} %get-tuple-element.246, bf16[256,2,128,1]{2,1,0,3:T(2,128)(2,1)S(1)} %bitcast.223, f32[256,2,4]{0,2,1:T(4,128)} %get-tuple-element.315, f32[2,256,256,4]{2,1,3,0:T(8,128)} %get-tuple-element.263, pred[256,256]{0,1:T(8,128)(4,1)S(1)} %bitcast.214), kind=kOutput, calls=%fused_computation.8 | convolution fusion | flops 137101312 | bytes 3358720 | tf_op jit(solution)/shard_map/cond/branch_1_fun/qhgk,khd->qhgd/dot_general | solution.py:47
  87.3 1.2 fusion.6
  88.5 0.7 fusion.16
  89.2 21.6 %conditional.5 = ((f32[256,2,4]{0,2,1:T(4,128)}, f32[256,2,4]{0,2,1:T(4,128)S(1)}, f32[256,2,4]{0,2,1:T(4,128)S(1)}, f32[256,2,4,128]{3,0,2,1:T(8,128)S(1)}, f32[256,2,4,128]{3,0,2,1:T(8,128)S(1)})) conditional(s32[]{:T(128)} %convert_element_type.54, (f32[256,2,4]{0,2,1:T(4,128)}, f32[256,2,4]{0,2,1:T(4,128)S(1)}, f32[256,2,4]{0,2,1:T(4,128)S(1)}, ...), branch_computations={%region_9.0_spmd, %region_10.14_spmd} | conditional | flops 820779008 | bytes 35913832 | solution.py:105
  89.4 0.9 reshape.534
  90.4 1.8 fusion.20
  92.9 1.7 fusion.32
  94.6 1.6 reshape.535
  96.2 4.2 %fusion.99 = (f32[256,2,4]{0,2,1:T(4,128)S(1)}, bf16[256,2,4,256]{0,3,2,1:T(8,128)(2,1)}) fusion(f32[2,256,256,4]{2,1,3,0:T(8,128)} %fusion.32, bf16[256,2,4,128]{0,3,2,1:T(8,128)(2,1)S(1)} %get-tuple-element.206, bf16[256,2,128,1]{2,1,0,3:T(2,128)(2,1)} %bitcast.239, f32[256,2,4]{0,2,1:T(4,128)S(1)} %max.6, f32[2,256,256,4]{2,1,3,0:T(8,128)} %get-tuple-element.267, ...), kind=kOutput, calls=%fused_computation.135 | convolution fusion | flops 138934272 | bytes 5980160 | tf_op jit(solution)/shard_map/cond/branch_1_fun/qhgd,khd->qhgk/dot_general | solution.py:36
  101.8 3.3 %fusion.27 = f32[2,256,4,128]{3,1,2,0:T(8,128)} fusion(bf16[256,2,128,1]{2,1,0,3:T(2,128)(2,1)} %bitcast.243, f32[256,2,4]{0,2,1:T(4,128)S(1)} %max.6, f32[2,256,256,4]{2,1,3,0:T(8,128)} %get-tuple-element.267, pred[256,256]{0,1:T(8,128)(4,1)S(1)} %bitcast.208), kind=kOutput, calls=%fused_computation.37 | convolution fusion | flops 136839168 | bytes 3350528 | tf_op jit(solution)/shard_map/cond/branch_1_fun/qhgk,khd->qhgd/dot_general | solution.py:48
  105.1 0.9 reshape.536
  106.1 2.5 %fusion.22 = f32[256,2,4,128]{3,0,2,1:T(8,128)S(1)} fusion(f32[2,256,4,128]{3,1,2,0:T(8,128)} %fusion.27, bf16[256,2,4,256]{0,3,2,1:T(8,128)(2,1)} %get-tuple-element.269, f32[256,2,4,128]{3,0,2,1:T(8,128)S(1)} %get-tuple-element.131, f32[256,2,4]{0,2,1:T(4,128)S(1)} %bitcast.249, bf16[256,2,128,1]{2,1,0,3:T(2,128)(2,1)S(1)} %bitcast.216), kind=kOutput, calls=%fused_computation.31 | convolution fusion | flops 135004160 | bytes 4333568 | tf_op jit(solution)/shard_map/cond/branch_1_fun/qhgk,khd->qhgd/dot_general | solution.py:50
  108.6 1.1 fusion.23
  110.9 3.9 %conditional.7 = (f32[256,2,4]{0,2,1:T(4,128)S(1)}, f32[256,2,4]{0,2,1:T(4,128)S(1)}, f32[256,2,4,128]{0,3,2,1:T(8,128)S(1)}, f32[256,2,4,128]{0,3,2,1:T(8,128)}) conditional(s32[]{:T(128)} %convert_element_type.52, (f32[256,2,4]{0,2,1:T(4,128)S(1)}, f32[256,2,4]{0,2,1:T(4,128)S(1)}, f32[256,2,4,128]{3,0,2,1:T(8,128)S(1)}, ...), branch_computations={%region_19.20_spmd, %region_20.24_spmd} | conditional | flops 820779008 | bytes 43761752 | solution.py:105
  110.9 1.0 copy-done.4
  111.9 1.6 copy.186
  113.4 1.3 copy.188
  114.8 1.5 subtract_convert_fusion
  116.3 7.1 %convolution_convert_fusion.1 = bf16[256,4096]{1,0:T(8,128)(2,1)} fusion(bf16[256,1024]{0,1:T(8,128)(2,1)S(1)} %bitcast.187, bf16[1024,4096]{1,0:T(8,128)(2,1)} %param.23), kind=kOutput, calls=%fused_computation.98 | convolution fusion | flops 2148532224 | bytes 11010048 | tf_op jit(solution)/shard_map/dot_general | solution.py:119
  123.4 7.1 %convolution_convert_fusion = bf16[256,4096]{1,0:T(8,128)(2,1)} fusion(bf16[256,1024]{0,1:T(8,128)(2,1)S(1)} %bitcast.186, bf16[1024,4096]{1,0:T(8,128)(2,1)} %param.23), kind=kOutput, calls=%fused_computation.97 | convolution fusion | flops 2148532224 | bytes 11010048 | tf_op jit(solution)/shard_map/dot_general | solution.py:120
  130.5 68.5 %reduce-scatter.3.cloned.1.call-done = bf16[256,1024]{1,0:T(8,128)(2,1)} async-done(((bf16[256,4096]{1,0:T(8,128)(2,1)}), bf16[256,1024]{1,0:T(8,128)(2,1)}) %reduce-scatter.3.cloned.1.call-update) | async-done | bytes 524304 | tf_op jit(solution)/shard_map/reduce_scatter | solution.py:122
  199.0 35.1 %reduce-scatter.5.cloned.1.call-done = bf16[256,1024]{1,0:T(8,128)(2,1)} async-done(((bf16[256,4096]{1,0:T(8,128)(2,1)}), bf16[256,1024]{1,0:T(8,128)(2,1)}) %reduce-scatter.5.cloned.1.call-update) | async-done | bytes 524304 | tf_op jit(solution)/shard_map/reduce_scatter | solution.py:125
  (59 shorter events, 4.8 us)
Async XLA Ops:
  7.2 59.0 %copy-start.15 = (s32[256]{0:T(256)S(1)}, s32[256]{0:T(256)}, u32[]{:S(2)}) copy-start(s32[256]{0:T(256)} %param.22) | copy-start | bytes 3076
  7.2 191.8 %reduce-scatter.3.cloned.1.call-start = ((), (), s32[]{:S(2)}) async-start(), calls=%async_computation.2 | async-start | bytes 2621440 | tf_op jit(solution)/shard_map/reduce_scatter | solution.py:122
  7.2 18.1 %collective-permute-start = (s32[256]{0:T(256)}, s32[256]{0:T(256)S(1)}, u32[]{:S(2)}, u32[]{:S(2)}) collective-permute-start(s32[256]{0:T(256)} %param.22), channel_id=1, source_target_pairs={{0,4},{4,8},{8,12},{12,16},{16,20},{20,24},{24,28},{28,32},{32,36}... | collective-permute-start | bytes 3080 | tf_op jit(solution)/shard_map/ppermute | solution.py:19
  10.6 23.9 %collective-permute-start.3 = (bf16[256,256]{1,0:T(8,128)(2,1)}, bf16[256,256]{1,0:T(8,128)(2,1)S(1)}, u32[]{:S(2)}, u32[]{:S(2)}) collective-permute-start(bf16[256,256]{1,0:T(8,128)(2,1)} %param.17), channel_id=1, source_target_pairs={{0,4},{4,8},{8,12},{12,16},{16,20},{20,24},{24,28},{28,32},{32,36}... | collective-permute-start | bytes 393224 | tf_op jit(solution)/shard_map/ppermute | solution.py:19
  14.0 22.9 %collective-permute-start.4 = (bf16[256,256]{1,0:T(8,128)(2,1)}, bf16[256,256]{1,0:T(8,128)(2,1)S(1)}, u32[]{:S(2)}, u32[]{:S(2)}) collective-permute-start(bf16[256,256]{1,0:T(8,128)(2,1)} %param.20), channel_id=1, source_target_pairs={{0,4},{4,8},{8,12},{12,16},{16,20},{20,24},{24,28},{28,32},{32,36}... | collective-permute-start | bytes 393224 | tf_op jit(solution)/shard_map/ppermute | solution.py:19
  17.2 23.2 %collective-permute-start.5 = (bf16[256,256]{1,0:T(8,128)(2,1)}, bf16[256,256]{1,0:T(8,128)(2,1)S(1)}, u32[]{:S(2)}, u32[]{:S(2)}) collective-permute-start(bf16[256,256]{1,0:T(8,128)(2,1)} %param.18), channel_id=1, source_target_pairs={{0,4},{4,8},{8,12},{12,16},{16,20},{20,24},{24,28},{28,32},{32,36}... | collective-permute-start | bytes 393224 | tf_op jit(solution)/shard_map/ppermute | solution.py:19
  21.9 10.7 %collective-permute-start.6 = (bf16[256,256]{1,0:T(8,128)(2,1)}, bf16[256,256]{1,0:T(8,128)(2,1)S(1)}, u32[]{:S(2)}, u32[]{:S(2)}) collective-permute-start(bf16[256,256]{1,0:T(8,128)(2,1)} %param.21), channel_id=1, source_target_pairs={{0,4},{4,8},{8,12},{12,16},{16,20},{20,24},{24,28},{28,32},{32,36}... | collective-permute-start | bytes 393224 | tf_op jit(solution)/shard_map/ppermute | solution.py:19
  25.3 24.4 %collective-permute-start.1 = (s32[256]{0:T(256)S(1)}, s32[256]{0:T(256)S(1)}, u32[]{:S(2)}, u32[]{:S(2)}) collective-permute-start(s32[256]{0:T(256)S(1)} %collective-permute-done), channel_id=1, source_target_pairs={{0,4},{4,8},{8,12},{12,16},{16,20},{20,24},{24,28},{28,32},{32,36}... | collective-permute-start | bytes 3080 | tf_op jit(solution)/shard_map/ppermute | solution.py:19
  32.6 37.5 %copy-start.13 = (bf16[256,256]{1,0:T(8,128)(2,1)}, bf16[256,256]{1,0:T(8,128)(2,1)S(1)}, u32[]{:S(2)}) copy-start(bf16[256,256]{1,0:T(8,128)(2,1)S(1)} %collective-permute-done.6) | copy-start | bytes 393220
  32.6 30.3 %collective-permute-start.10 = (bf16[256,256]{1,0:T(8,128)(2,1)S(1)}, bf16[256,256]{1,0:T(8,128)(2,1)}, u32[]{:S(2)}, u32[]{:S(2)}) collective-permute-start(bf16[256,256]{1,0:T(8,128)(2,1)S(1)} %collective-permute-done.6), channel_id=1, source_target_pairs={{0,4},{4,8},{8,12},{12,16},{16,20},{20,24},{24,28},{28,32},{32,36}... | collective-permute-start | bytes 393224 | tf_op jit(solution)/shard_map/ppermute | solution.py:19
  34.5 35.6 %copy-start.10 = (bf16[256,256]{1,0:T(8,128)(2,1)}, bf16[256,256]{1,0:T(8,128)(2,1)S(1)}, u32[]{:S(2)}) copy-start(bf16[256,256]{1,0:T(8,128)(2,1)S(1)} %collective-permute-done.3) | copy-start | bytes 393220
  34.5 19.7 %collective-permute-start.7 = (bf16[256,256]{1,0:T(8,128)(2,1)S(1)}, bf16[256,256]{1,0:T(8,128)(2,1)}, u32[]{:S(2)}, u32[]{:S(2)}) collective-permute-start(bf16[256,256]{1,0:T(8,128)(2,1)S(1)} %collective-permute-done.3), channel_id=1, source_target_pairs={{0,4},{4,8},{8,12},{12,16},{16,20},{20,24},{24,28},{28,32},{32,36}... | collective-permute-start | bytes 393224 | tf_op jit(solution)/shard_map/ppermute | solution.py:19
  36.9 33.2 %copy-start.11 = (bf16[256,256]{1,0:T(8,128)(2,1)}, bf16[256,256]{1,0:T(8,128)(2,1)S(1)}, u32[]{:S(2)}) copy-start(bf16[256,256]{1,0:T(8,128)(2,1)S(1)} %collective-permute-done.4) | copy-start | bytes 393220
  36.9 19.2 %collective-permute-start.8 = (bf16[256,256]{1,0:T(8,128)(2,1)S(1)}, bf16[256,256]{1,0:T(8,128)(2,1)}, u32[]{:S(2)}, u32[]{:S(2)}) collective-permute-start(bf16[256,256]{1,0:T(8,128)(2,1)S(1)} %collective-permute-done.4), channel_id=1, source_target_pairs={{0,4},{4,8},{8,12},{12,16},{16,20},{20,24},{24,28},{28,32},{32,36}... | collective-permute-start | bytes 393224 | tf_op jit(solution)/shard_map/ppermute | solution.py:19
  40.4 29.8 %copy-start.12 = (bf16[256,256]{1,0:T(8,128)(2,1)}, bf16[256,256]{1,0:T(8,128)(2,1)S(1)}, u32[]{:S(2)}) copy-start(bf16[256,256]{1,0:T(8,128)(2,1)S(1)} %collective-permute-done.5) | copy-start | bytes 393220
  40.4 17.7 %collective-permute-start.9 = (bf16[256,256]{1,0:T(8,128)(2,1)S(1)}, bf16[256,256]{1,0:T(8,128)(2,1)}, u32[]{:S(2)}, u32[]{:S(2)}) collective-permute-start(bf16[256,256]{1,0:T(8,128)(2,1)S(1)} %collective-permute-done.5), channel_id=1, source_target_pairs={{0,4},{4,8},{8,12},{12,16},{16,20},{20,24},{24,28},{28,32},{32,36}... | collective-permute-start | bytes 393224 | tf_op jit(solution)/shard_map/ppermute | solution.py:19
  49.7 16.4 %collective-permute-start.2 = (s32[256]{0:T(256)S(1)}, s32[256]{0:T(256)S(1)}, u32[]{:S(2)}, u32[]{:S(2)}) collective-permute-start(s32[256]{0:T(256)S(1)} %collective-permute-done.1), channel_id=1, source_target_pairs={{0,4},{4,8},{8,12},{12,16},{16,20},{20,24},{24,28},{28,32},{32,36}... | collective-permute-start | bytes 3080 | tf_op jit(solution)/shard_map/ppermute | solution.py:19
  54.2 56.7 %collective-permute-start.11 = (bf16[256,256]{1,0:T(8,128)(2,1)}, bf16[256,256]{1,0:T(8,128)(2,1)}, u32[]{:S(2)}, u32[]{:S(2)}) collective-permute-start(bf16[256,256]{1,0:T(8,128)(2,1)} %collective-permute-done.7), channel_id=1, source_target_pairs={{0,4},{4,8},{8,12},{12,16},{16,20},{20,24},{24,28},{28,32},{32,36}... | collective-permute-start | bytes 393224 | tf_op jit(solution)/shard_map/ppermute | solution.py:19
  56.1 54.7 %collective-permute-start.12 = (bf16[256,256]{1,0:T(8,128)(2,1)}, bf16[256,256]{1,0:T(8,128)(2,1)}, u32[]{:S(2)}, u32[]{:S(2)}) collective-permute-start(bf16[256,256]{1,0:T(8,128)(2,1)} %collective-permute-done.8), channel_id=1, source_target_pairs={{0,4},{4,8},{8,12},{12,16},{16,20},{20,24},{24,28},{28,32},{32,36}... | collective-permute-start | bytes 393224 | tf_op jit(solution)/shard_map/ppermute | solution.py:19
  58.1 52.8 %collective-permute-start.13 = (bf16[256,256]{1,0:T(8,128)(2,1)}, bf16[256,256]{1,0:T(8,128)(2,1)}, u32[]{:S(2)}, u32[]{:S(2)}) collective-permute-start(bf16[256,256]{1,0:T(8,128)(2,1)} %collective-permute-done.9), channel_id=1, source_target_pairs={{0,4},{4,8},{8,12},{12,16},{16,20},{20,24},{24,28},{28,32},{32,36}... | collective-permute-start | bytes 393224 | tf_op jit(solution)/shard_map/ppermute | solution.py:19
  62.9 48.0 %collective-permute-start.14 = (bf16[256,256]{1,0:T(8,128)(2,1)}, bf16[256,256]{1,0:T(8,128)(2,1)}, u32[]{:S(2)}, u32[]{:S(2)}) collective-permute-start(bf16[256,256]{1,0:T(8,128)(2,1)} %collective-permute-done.10), channel_id=1, source_target_pairs={{0,4},{4,8},{8,12},{12,16},{16,20},{20,24},{24,28},{28,32},{32,36}... | collective-permute-start | bytes 393224 | tf_op jit(solution)/shard_map/ppermute | solution.py:19
  72.9 2.3 copy-start.7
  75.3 3.2 %copy-start.9 = (bf16[256,256]{1,0:T(8,128)(2,1)S(1)}, bf16[256,256]{1,0:T(8,128)(2,1)}, u32[]{:S(2)}) copy-start(bf16[256,256]{1,0:T(8,128)(2,1)} %get-tuple-element.120) | copy-start | bytes 393220 | tf_op jit(solution)/shard_map/cond
  78.6 3.4 %copy-start.8 = (bf16[256,256]{1,0:T(8,128)(2,1)S(1)}, bf16[256,256]{1,0:T(8,128)(2,1)}, u32[]{:S(2)}) copy-start(bf16[256,256]{1,0:T(8,128)(2,1)} %get-tuple-element.119) | copy-start | bytes 393220 | tf_op jit(solution)/shard_map/cond
  82.7 2.0 copy-start.6
  84.6 2.7 %copy-start.3 = (f32[2,256,256,4]{2,1,3,0:T(8,128)S(1)}, f32[2,256,256,4]{2,1,3,0:T(8,128)}, u32[]{:S(2)}) copy-start(f32[2,256,256,4]{2,1,3,0:T(8,128)} %get-tuple-element.263) | copy-start | bytes 6291460 | tf_op jit(solution)/shard_map/cond
  96.2 4.9 %copy-start.14 = (bf16[256,256]{1,0:T(8,128)(2,1)S(1)}, bf16[256,256]{1,0:T(8,128)(2,1)}, u32[]{:S(2)}) copy-start(bf16[256,256]{1,0:T(8,128)(2,1)} %get-tuple-element.132) | copy-start | bytes 393220 | tf_op jit(solution)/shard_map/cond
  106.1 2.6 %copy-start.1 = (f32[2,256,256,4]{2,1,3,0:T(8,128)S(1)}, f32[2,256,256,4]{2,1,3,0:T(8,128)}, u32[]{:S(2)}) copy-start(f32[2,256,256,4]{2,1,3,0:T(8,128)} %get-tuple-element.267) | copy-start | bytes 6291460 | tf_op jit(solution)/shard_map/cond
  110.9 1.0 copy-start.4
  123.4 110.7 %reduce-scatter.5.cloned.1.call-start = ((), (), s32[]{:S(2)}) async-start(), calls=%async_computation.3 | async-start | bytes 2621440 | tf_op jit(solution)/shard_map/reduce_scatter | solution.py:125
Sparse Core Ops, SparseCore 0:
  123.5 75.4 reduce-scatter.2
  202.3 31.7 reduce-scatter.4
where the time goes:
time: 245 us; the launch traced here: 241 us
  waiting for transfers between devices  107 us (44%)
  starting transfers between devices  52.4 us (21%)
  matrix products  43.6 us (18%)
  between operations  16.9 us (7%)
  local copies, waits for them, and re-layouts  12.8 us (5%)
  other arithmetic  7.37 us (3%)
    reduce_scatter x1, waiting for transfers between devices, per_device(): lax.psum_scatter(out_term.astype(jnp.bfloat16), 'head', scatter_dimension...  68.5 us
    ppermute x15, starting transfers between devices, passed_along(): lax.ppermute(value, axis, [(source, source + steps) for source in range(l...  52.3 us
    reduce_scatter x1, waiting for transfers between devices, per_device(): lax.psum_scatter(tan_term.astype(jnp.bfloat16), 'head', scatter_dimension...  35.1 us
    dot_general x2, matrix products, score_pair(): jnp.einsum('qhgd,khd->qhgk', q_heads, kt_heads, preferred_element_type=jn...  7.4 us
    dot_general x1, matrix products, per_device(): jnp.dot(attended_rows, out_weight, preferred_element_type=jnp.float32)  7.09 us
    dot_general x1, matrix products, per_device(): jnp.dot(tangent_rows, out_weight, preferred_element_type=jnp.float32)  7.08 us
    dot_general x2, matrix products, accumulate(): jnp.einsum('qhgk,khd->qhgd', rounded, vt_heads, preferred_element_type=jn...  6.74 us
    reshape x8, local copies, waits for them, and re-layouts, key_view(): return block.reshape(block.shape[0], block.shape[1] // HD, HD)  5.83 us
  transfers between devices with their start and end apart: 17, of which 3 were waited for; matrix products, arithmetic and copies ran while one was open for 21% of the time, Pallas kernels for 0%

commit v1 on v0

v1 whole, which is shorter than its diff:
```python
import functools
import math

import jax
import jax.numpy as jnp
from jax import lax
from jax.experimental import pallas as pl
from jax.experimental.pallas import tpu as pltpu
from jax.sharding import PartitionSpec as P

HD = 128
ROWS = 256
LANES = 128
TILE = 64
TILES = ROWS // TILE
GROUP = 4
KV_LOCAL = 2
RING = 4
WIDE = 1024
PIECE = 512
PIECES = WIDE // PIECE
CHUNKS = 8
PART = ROWS // CHUNKS
CHUNK_ROWS = 4 * PART + 16
SLOTS = 6
HANDS = 2
FILL = -3e38
SCALE = 1.0 / math.sqrt(HD)
LOG2E = math.log2(math.e)
MESH = pl.DeviceIdType.MESH
F32 = jnp.float32
BF16 = jnp.bfloat16


SEND, WAIT = 0, 1
ALL, INNER, OUTER = 0, 1, 2
SCRIPT = (
    (
        (
            (SEND, 0, 1, 0, 1, ALL),
            (SEND, 0, 3, 0, 3, ALL),
            (SEND, 0, 1, 1, 1, ALL),
            (SEND, 0, 3, 1, 3, ALL),
            (SEND, 0, 1, 2, 1, ALL),
            (SEND, 0, 3, 2, 3, ALL),
            (SEND, 0, 1, 3, 1, ALL),
            (SEND, 0, 3, 3, 3, ALL),
            (SEND, 0, 1, 4, 1, ALL),
            (SEND, 0, 1, 5, 1, ALL),
            (SEND, 0, 1, 6, 1, ALL),
            (SEND, 0, 1, 7, 1, ALL),
        ),
        (
            (WAIT, 4, 0, ALL),
            (SEND, 4, 2, 0, 3, ALL),
            (SEND, 4, 3, 0, 4, OUTER),
            (WAIT, 5, 5, OUTER),
            (SEND, 5, 2, 5, 4, OUTER),
            (WAIT, 4, 1, ALL),
            (SEND, 4, 2, 1, 3, ALL),
            (SEND, 4, 3, 1, 4, OUTER),
            (WAIT, 5, 6, OUTER),
            (SEND, 5, 2, 6, 4, OUTER),
            (WAIT, 4, 2, ALL),
            (SEND, 4, 2, 2, 3, ALL),
            (SEND, 4, 3, 2, 4, OUTER),
            (WAIT, 5, 7, OUTER),
            (SEND, 5, 2, 7, 4, OUTER),
            (WAIT, 4, 3, ALL),
            (SEND, 4, 2, 3, 3, ALL),
            (SEND, 4, 3, 3, 4, OUTER),
            (WAIT, 1, 0, INNER),
            (SEND, 1, 2, 0, 1, INNER),
            (WAIT, 4, 4, ALL),
            (SEND, 4, 2, 4, 3, ALL),
            (SEND, 4, 3, 4, 4, OUTER),
            (WAIT, 1, 1, INNER),
            (SEND, 1, 2, 1, 1, INNER),
            (WAIT, 4, 5, ALL),
            (SEND, 4, 2, 5, 3, ALL),
            (SEND, 4, 3, 5, 4, OUTER),
            (SEND, 0, 3, 4, 3, ALL),
            (SEND, 0, 3, 5, 3, ALL),
            (SEND, 0, 3, 6, 3, ALL),
            (SEND, 0, 3, 7, 3, ALL),
            (WAIT, 1, 2, INNER),
            (SEND, 1, 2, 2, 1, INNER),
            (WAIT, 4, 6, OUTER),
            (SEND, 4, 3, 6, 4, OUTER),
            (WAIT, 1, 3, INNER),
            (SEND, 1, 2, 3, 1, INNER),
            (WAIT, 4, 7, OUTER),
            (SEND, 4, 3, 7, 4, OUTER),
            (WAIT, 1, 4, INNER),
            (SEND, 1, 2, 4, 1, INNER),
        ),
        (
        ),
    ),
    (
        (
            (SEND, 0, 1, 0, 2, ALL),
            (SEND, 0, 4, 0, 0, ALL),
            (SEND, 0, 1, 1, 2, ALL),
            (SEND, 0, 4, 1, 0, ALL),
            (SEND, 0, 1, 2, 2, ALL),
            (SEND, 0, 4, 2, 0, ALL),
            (SEND, 0, 1, 3, 2, ALL),
            (SEND, 0, 4, 3, 0, ALL),
            (SEND, 0, 1, 4, 2, ALL),
            (SEND, 0, 4, 4, 0, ALL),
            (SEND, 0, 1, 5, 2, ALL),
            (SEND, 0, 4, 5, 0, ALL),
            (SEND, 0, 1, 6, 2, ALL),
            (SEND, 0, 4, 6, 0, OUTER),
            (SEND, 0, 1, 7, 2, ALL),
            (SEND, 0, 4, 7, 0, OUTER),
        ),
        (
            (WAIT, 4, 5, OUTER),
            (SEND, 4, 2, 5, 4, OUTER),
            (WAIT, 4, 6, OUTER),
            (SEND, 4, 2, 6, 4, OUTER),
            (WAIT, 4, 7, OUTER),
            (SEND, 4, 2, 7, 4, OUTER),
            (WAIT, 3, 0, INNER),
            (SEND, 3, 2, 0, 0, INNER),
            (WAIT, 1, 4, ALL),
            (SEND, 1, 2, 4, 2, ALL),
            (WAIT, 3, 1, INNER),
            (SEND, 3, 2, 1, 0, INNER),
            (WAIT, 1, 5, ALL),
            (SEND, 1, 2, 5, 2, ALL),
            (WAIT, 3, 2, INNER),
            (SEND, 3, 2, 2, 0, INNER),
            (WAIT, 1, 6, ALL),
            (SEND, 1, 2, 6, 2, ALL),
            (WAIT, 3, 3, INNER),
            (SEND, 3, 2, 3, 0, INNER),
            (WAIT, 1, 7, ALL),
            (SEND, 1, 2, 7, 2, ALL),
            (WAIT, 3, 4, INNER),
            (SEND, 3, 2, 4, 0, INNER),
        ),
        (
        ),
    ),
    (
        (
            (SEND, 0, 5, 5, 0, OUTER),
            (SEND, 0, 5, 6, 0, OUTER),
            (SEND, 0, 5, 7, 0, OUTER),
            (SEND, 0, 4, 0, 4, OUTER),
            (SEND, 0, 1, 0, 3, ALL),
            (SEND, 0, 4, 1, 4, OUTER),
            (SEND, 0, 1, 1, 3, ALL),
            (SEND, 0, 4, 2, 4, OUTER),
            (SEND, 0, 1, 2, 3, ALL),
            (SEND, 0, 4, 3, 4, OUTER),
            (SEND, 0, 1, 3, 3, ALL),
            (SEND, 0, 4, 4, 4, OUTER),
            (SEND, 0, 1, 4, 3, ALL),
            (SEND, 0, 4, 5, 4, OUTER),
            (SEND, 0, 1, 5, 3, ALL),
            (SEND, 0, 4, 6, 4, OUTER),
            (SEND, 0, 1, 6, 3, ALL),
            (SEND, 0, 4, 7, 4, OUTER),
            (SEND, 0, 1, 7, 3, ALL),
        ),
        (
            (WAIT, 4, 0, INNER),
            (SEND, 4, 3, 0, 1, INNER),
            (WAIT, 4, 1, INNER),
            (SEND, 4, 3, 1, 1, INNER),
            (WAIT, 4, 2, INNER),
            (SEND, 4, 3, 2, 1, INNER),
            (WAIT, 4, 3, INNER),
            (SEND, 4, 3, 3, 1, INNER),
            (WAIT, 4, 4, INNER),
            (SEND, 4, 3, 4, 1, INNER),
            (WAIT, 4, 5, INNER),
            (SEND, 4, 3, 5, 1, INNER),
            (WAIT, 1, 6, ALL),
            (SEND, 1, 2, 6, 3, ALL),
            (WAIT, 4, 6, INNER),
            (SEND, 4, 3, 6, 1, INNER),
            (WAIT, 1, 7, ALL),
            (SEND, 1, 2, 7, 3, ALL),
            (WAIT, 4, 7, INNER),
            (SEND, 4, 3, 7, 1, INNER),
        ),
        (
        ),
    ),
    (
        (
            (SEND, 0, 4, 5, 1, OUTER),
            (SEND, 0, 4, 6, 1, OUTER),
            (SEND, 0, 4, 7, 1, OUTER),
            (SEND, 0, 4, 0, 4, OUTER),
            (SEND, 0, 4, 1, 4, OUTER),
            (SEND, 0, 4, 2, 4, OUTER),
            (SEND, 0, 4, 3, 4, OUTER),
            (SEND, 0, 4, 4, 4, OUTER),
            (SEND, 0, 4, 5, 4, OUTER),
            (SEND, 0, 4, 6, 4, OUTER),
            (SEND, 0, 4, 7, 4, OUTER),
        ),
        (
            (WAIT, 3, 0, ALL),
            (SEND, 3, 2, 0, 2, ALL),
            (WAIT, 4, 0, INNER),
            (SEND, 4, 1, 0, 0, INNER),
            (SEND, 4, 3, 0, 2, INNER),
            (WAIT, 3, 1, ALL),
            (SEND, 3, 2, 1, 2, ALL),
            (WAIT, 4, 1, INNER),
            (SEND, 4, 1, 1, 0, INNER),
            (SEND, 4, 3, 1, 2, INNER),
            (WAIT, 3, 2, ALL),
            (SEND, 3, 2, 2, 2, ALL),
            (WAIT, 4, 2, INNER),
            (SEND, 4, 1, 2, 0, INNER),
            (SEND, 4, 3, 2, 2, INNER),
            (WAIT, 3, 3, ALL),
            (SEND, 3, 2, 3, 2, ALL),
            (WAIT, 4, 3, INNER),
            (SEND, 4, 1, 3, 0, INNER),
            (SEND, 4, 3, 3, 2, INNER),
            (WAIT, 4, 4, INNER),
            (SEND, 4, 1, 4, 0, INNER),
            (SEND, 4, 3, 4, 2, INNER),
            (WAIT, 4, 5, INNER),
            (SEND, 4, 1, 5, 0, INNER),
            (SEND, 4, 3, 5, 2, INNER),
            (WAIT, 4, 6, INNER),
            (SEND, 4, 1, 6, 0, INNER),
            (SEND, 4, 3, 6, 2, INNER),
            (WAIT, 4, 7, INNER),
            (SEND, 4, 1, 7, 0, INNER),
            (SEND, 4, 3, 7, 2, INNER),
        ),
        (
        ),
    ),
)
MOST = max(sum(op[0] == SEND for phase in script for op in phase) for script in SCRIPT)


def dot(a, b):
    return lax.dot_general(a, b, (((1,), (0,)), ((), ())), preferred_element_type=F32)


def dot_t(a, b):
    return lax.dot_general(a, b, (((1,), (1,)), ((), ())), preferred_element_type=F32)


def both(a):
    return jnp.concatenate([a, a], axis=-1)


def kernel(
    n_seq,
    q_hbm, k_hbm, v_hbm, qt_hbm, kt_hbm, vt_hbm, seg_ref, w_hbm,
    out_hbm, tan_hbm,
    qbuf, qtbuf, kv, wbuf, att, rs_out, rs_in, own, acc, tsum, mref, lref, out_ref, tan_ref,
    load_sem, q_sem, w_sem, wx_send, wx_recv, halo_send, halo_recv,
    att_send, att_recv, rs_send, rs_recv, store_sem,
):
    seq = lax.axis_index("seq")
    head = lax.axis_index("head")
    x = lax.rem(seq, RING)
    base = seq - x
    not_first = seq >= RING
    not_last = seq < n_seq - RING
    core = lax.rem(head, 2)
    y_lo = head // 2
    other_core = {"seq": seq, "head": y_lo * 2 + 1 - core}
    other_chip = {"seq": seq, "head": (1 - y_lo) * 2 + core}
    peers = [{"seq": base + lax.rem(x + d, RING), "head": head} for d in (1, 2, 3)]
    after = {"seq": lax.rem(seq + RING, n_seq), "head": head}
    before = {"seq": lax.rem(seq + n_seq - RING, n_seq), "head": head}

    barrier = pltpu.get_barrier_semaphore()
    for target in (*peers, before, other_core, other_chip):
        pl.semaphore_signal(barrier, inc=1, device_id=target, device_id_type=MESH)

    kv_loads = []
    for a, ref in enumerate((k_hbm, kt_hbm, v_hbm, vt_hbm)):
        kv_loads.append(
            pltpu.make_async_copy(ref, kv.at[0, :, pl.ds(a * PART, PART)], load_sem.at[a])
        )
    q_loads = [
        pltpu.make_async_copy(q_hbm, qbuf, q_sem.at[0]),
        pltpu.make_async_copy(qt_hbm, qtbuf, q_sem.at[1]),
    ]
    w_loads = []
    for yb in range(2):
        w_loads.append(
            pltpu.make_async_copy(
                w_hbm.at[:, pl.ds(pl.multiple_of((yb * 2 + core) * WIDE, WIDE), WIDE)],
                wbuf.at[core, yb],
                w_sem.at[yb],
            )
        )
    for load in kv_loads + q_loads:
        load.start()

    seg_row = seg_ref[...].astype(F32)
    kv[0, CHUNKS - 1, 4 * PART :, :] = jnp.broadcast_to(seg_row, (16, ROWS)).astype(BF16)
    for load in kv_loads:
        load.wait()
    pl.semaphore_wait(barrier, 6)

    def remote(src, dst, send, recv, target):
        return pltpu.make_async_remote_copy(
            src_ref=src, dst_ref=dst, send_sem=send, recv_sem=recv,
            device_id=target, device_id_type=MESH,
        )

    def flagged(flag, act):
        if flag:
            pl.when(not_first if flag == INNER else not_last)(act)
        else:
            act()

    def halo(src, dst, c, index, target):
        place = after if target == RING else {"seq": base + target, "head": head}
        rows = pl.ds(0, CHUNK_ROWS if c == 0 else 4 * PART)
        return remote(
            kv.at[src, CHUNKS - 1 - c, rows], kv.at[dst, CHUNKS - 1 - c, rows],
            halo_send.at[index], halo_recv.at[dst - 1, c], place,
        )

    def got(slot, c):
        halo(0, slot, c, 0, RING).wait_recv()

    def run(phase):
        for at in range(RING):
            @pl.when(x == at)
            def _():
                index = sum(op[0] == SEND for done in SCRIPT[at][:phase] for op in done)
                for op in SCRIPT[at][phase]:
                    if op[0] == SEND:
                        _, src, dst, c, target, flag = op
                        flagged(flag, halo(src, dst, c, index, target).start)
                        index += 1
                    else:
                        _, slot, c, flag = op
                        flagged(flag, functools.partial(got, slot, c))

    run(0)

    w_swaps = []
    for yb in range(2):
        w_swaps.append(
            remote(
                w_hbm.at[:, pl.ds(pl.multiple_of((yb * 2 + 1 - core) * WIDE, WIDE), WIDE)],
                wbuf.at[core, yb],
                wx_send.at[yb],
                wx_recv.at[yb],
                other_core,
            )
        )
    for copy in w_swaps + w_loads:
        copy.start()

    def arrive(slot, chunks):
        for at in range(RING):
            seen = {op[1:3] for phase in SCRIPT[at] for op in phase if op[0] == WAIT}
            left = [c for c in chunks if (slot, c) not in seen]
            if left:
                @pl.when((x == at) & (seq >= slot))
                def _():
                    for c in left:
                        got(slot, c)

    row_id = lax.broadcasted_iota(jnp.int32, (TILE, ROWS), 0)
    col_id = lax.broadcasted_iota(jnp.int32, (TILE, ROWS), 1)

    def seg_column(tile):
        spread = jnp.where(row_id + tile * TILE == col_id, jnp.broadcast_to(seg_row, (TILE, ROWS)), 0.0)
        return jnp.sum(spread, axis=1, keepdims=True)

    seg_q = [seg_column(tile) for tile in range(TILES)]

    def fold(tile, slot, chunks, first=False):
        if not first:
            @pl.when(seq >= slot)
            def _():
                fold_in(tile, slot, chunks, False)
        else:
            fold_in(tile, slot, chunks, True)

    def fold_in(tile, slot, chunks, first):
        width = PART * len(chunks)
        begin = (CHUNKS - 1 - chunks[0]) * PART
        rows = slice(tile * TILE, (tile + 1) * TILE)
        seg_k = kv[slot, CHUNKS - 1, 4 * PART : 4 * PART + 16, :].astype(F32)[0:1, begin : begin + width]
        ok = jnp.broadcast_to(seg_q[tile], (TILE, width)) == jnp.broadcast_to(seg_k, (TILE, width))
        if slot in (0, 3):
            row_at = lax.broadcasted_iota(jnp.int32, (TILE, width), 0) + tile * TILE
            col_at = lax.broadcasted_iota(jnp.int32, (TILE, width), 1) + begin
            ok = ok & ((col_at <= row_at) if slot == 0 else (col_at > row_at))
        bias = jnp.where(ok, 0.0, FILL)

        def block(a, g):
            return jnp.concatenate(
                [
                    kv[slot, CHUNKS - 1 - c, a * PART : (a + 1) * PART, g * HD : (g + 1) * HD]
                    for c in chunks
                ],
                axis=0,
            )

        for g in range(KV_LOCAL):
            heads = [slice((g * GROUP + j) * HD, (g * GROUP + j + 1) * HD) for j in range(GROUP)]
            qs = jnp.concatenate([qbuf[rows, h] for h in heads], axis=0)
            qts = jnp.concatenate([qtbuf[rows, h] for h in heads], axis=0)
            k, kt, v, vt = (block(a, g) for a in range(4))
            s = dot_t(qs, k)
            t = dot_t(jnp.concatenate([qts, qs], axis=1), jnp.concatenate([k, kt], axis=1))
            s = (s * (SCALE * LOG2E)).reshape(GROUP, TILE, width) + bias[None]
            s = s.reshape(GROUP * TILE, width)
            top = jnp.max(s, axis=1, keepdims=True)
            if first:
                m_new = jnp.broadcast_to(top, (GROUP * TILE, HD))
            else:
                m_old = mref[tile, g]
                m_new = jnp.maximum(m_old, top)
                alpha = jnp.exp2(m_old - m_new)
            mref[tile, g] = m_new
            p = jnp.exp2(s - (both(m_new) if width == 2 * LANES else m_new))
            l = p[:, :LANES] + p[:, LANES:] if width == 2 * LANES else p
            wt = (p * (t * SCALE)).astype(BF16)
            pb = p.astype(BF16)
            o = dot(pb, jnp.concatenate([v, vt], axis=1))
            o2 = dot(wt, jnp.concatenate([v, jnp.ones((width, HD), BF16)], axis=1))
            tan = o[:, HD:] + o2[:, :HD]
            if first:
                lref[tile, g] = l
                acc[tile, g, :, 0:HD] = o[:, :HD]
                acc[tile, g, :, HD:] = tan
                tsum[tile, g] = o2[:, HD:]
            else:
                lref[tile, g] = lref[tile, g] * alpha + l
                acc[tile, g, :, 0:HD] = acc[tile, g, :, 0:HD] * alpha + o[:, :HD]
                acc[tile, g, :, HD:] = acc[tile, g, :, HD:] * alpha + tan
                tsum[tile, g] = tsum[tile, g] * alpha + o2[:, HD:]

    def finish(tile):
        for g in range(KV_LOCAL):
            finish_one(tile, g)
            att_copy(tile, g).start()

    def finish_one(tile, g):
        total = jnp.sum(lref[tile, g], axis=1, keepdims=True)
        inv = jnp.broadcast_to(1.0 / total, (GROUP * TILE, HD))
        mixed = acc[tile, g, :, 0:HD] * inv
        tangent = acc[tile, g, :, HD:] * inv - (tsum[tile, g] * inv) * mixed
        mixed = mixed.astype(BF16)
        tangent = tangent.astype(BF16)
        for j in range(GROUP):
            lanes = slice(j * HD, (j + 1) * HD)
            att[tile, core, g, 0:TILE, lanes] = mixed[j * TILE : (j + 1) * TILE]
            att[tile, core, g, TILE:, lanes] = tangent[j * TILE : (j + 1) * TILE]

    def att_copy(tile, g):
        return remote(
            att.at[tile, core, g], att.at[tile, core, g],
            att_send.at[tile, g], att_recv.at[tile, g], other_core,
        )

    def swapped(tile):
        for g in range(KV_LOCAL):
            att_copy(tile, g).wait_recv()

    def rs_copy(tile, n):
        return remote(
            rs_out.at[tile, n], rs_in.at[tile, n], rs_send.at[tile, n], rs_recv.at[tile, n], other_chip
        )

    def project(tile, yb, n):
        lanes = slice(n * PIECE, (n + 1) * PIECE)
        total = None
        for c in range(2):
            left = jnp.concatenate([att[tile, c, g] for g in range(KV_LOCAL)], axis=1)
            part = dot(left, wbuf[c, yb, :, lanes])
            total = part if total is None else total + part
        return total

    def send_parts(tile):
        for n in range(PIECES):
            rs_out[tile, n] = project(tile, 1 - y_lo, n).astype(BF16)
            rs_copy(tile, n).start()

    def own_parts(tile):
        for n in range(PIECES):
            own[tile, n] = project(tile, y_lo, n)

    def stores(tile, n):
        part = (pl.ds(tile * TILE, TILE), pl.ds(n * PIECE, PIECE))
        return [
            pltpu.make_async_copy(out_ref.at[part], out_hbm.at[part], store_sem.at[tile, n, 0]),
            pltpu.make_async_copy(tan_ref.at[part], tan_hbm.at[part], store_sem.at[tile, n, 1]),
        ]

    def final(tile):
        rows = slice(tile * TILE, (tile + 1) * TILE)
        for n in range(PIECES):
            rs_copy(tile, n).wait_recv()
            total = (own[tile, n] + rs_in[tile, n].astype(F32)).astype(BF16)
            lanes = slice(n * PIECE, (n + 1) * PIECE)
            out_ref[rows, lanes] = total[:TILE]
            tan_ref[rows, lanes] = total[TILE:]
            for copy in stores(tile, n):
                copy.start()

    every = tuple(range(CHUNKS - 1, -1, -1))
    low, high = every[: CHUNKS // 2], every[CHUNKS // 2 :]
    for load in q_loads:
        load.wait()
    for tile in (3, 2, 1, 0):
        fold(tile, 0, every if tile >= 2 else low, first=True)
    run(1)
    for copy in w_swaps:
        copy.wait_recv()
    for copy in w_loads:
        copy.wait()
    arrive(1, every)
    fold(3, 1, every)
    arrive(3, high)
    fold(3, 3, high)
    arrive(2, every)
    fold(3, 2, every)
    finish(3)
    fold(2, 1, every)
    fold(2, 3, high)
    fold(2, 2, every)
    finish(2)
    swapped(3)
    send_parts(3)
    fold(1, 1, every)
    fold(1, 2, every)
    swapped(2)
    send_parts(2)
    arrive(3, low)
    fold(1, 3, every)
    finish(1)
    fold(0, 1, every)
    fold(0, 2, every)
    swapped(1)
    send_parts(1)
    fold(0, 3, every)
    finish(0)
    own_parts(3)
    own_parts(2)
    swapped(0)
    send_parts(0)
    own_parts(1)
    own_parts(0)
    for tile in (3, 2, 1, 0):
        final(tile)

    for at in range(RING):
        @pl.when(x == at)
        def _():
            index = 0
            for op in (op for phase in SCRIPT[at] for op in phase if op[0] == SEND):
                _, src, dst, c, target, flag = op
                flagged(flag, halo(src, dst, c, index, target).wait_send)
                index += 1
    for copy in w_swaps:
        copy.wait_send()
    for tile in range(TILES):
        for g in range(KV_LOCAL):
            att_copy(tile, g).wait_send()
        for n in range(PIECES):
            rs_copy(tile, n).wait_send()
            for copy in stores(tile, n):
                copy.wait()


def copy_kernel(a_hbm, b_hbm, c_hbm, d_hbm, a_buf, b_buf, load_sem, store_sem):
    loads, stores = [], []
    for i in range(HANDS):
        rows = pl.ds(i * ROWS // HANDS, ROWS // HANDS)
        for j, (src, buf, dst) in enumerate(((a_hbm, a_buf, c_hbm), (b_hbm, b_buf, d_hbm))):
            loads.append(pltpu.make_async_copy(src.at[rows], buf.at[rows], load_sem.at[i, j]))
            stores.append(pltpu.make_async_copy(buf.at[rows], dst.at[rows], store_sem.at[i, j]))
    for load in loads:
        load.start()
    for load, store in zip(loads, stores):
        load.wait()
        store.start()
    for store in stores:
        store.wait()


def solution(mesh):
    n_seq = mesh.shape["seq"]

    def per_device(q, k, v, qt, kt, vt, seg, w):
        dma = pltpu.SemaphoreType.DMA
        anywhere = pl.BlockSpec(memory_space=pl.ANY)
        vmem = pl.BlockSpec(memory_space=pltpu.VMEM)
        stats = (TILES, KV_LOCAL, GROUP * TILE, HD)
        results = [jax.ShapeDtypeStruct((ROWS, WIDE), BF16)] * 2
        outs = pl.pallas_call(
            functools.partial(kernel, n_seq),
            out_shape=results,
            in_specs=[anywhere] * 6 + [vmem, anywhere],
            out_specs=[anywhere, anywhere],
            scratch_shapes=[
                pltpu.VMEM((ROWS, WIDE), BF16),
                pltpu.VMEM((ROWS, WIDE), BF16),
                pltpu.VMEM((SLOTS, CHUNKS, CHUNK_ROWS, 2 * HD), BF16),
                pltpu.VMEM((2, 2, WIDE, WIDE), BF16),
                pltpu.VMEM((TILES, 2, KV_LOCAL, 2 * TILE, WIDE // KV_LOCAL), BF16),
                pltpu.VMEM((TILES, PIECES, 2 * TILE, PIECE), BF16),
                pltpu.VMEM((TILES, PIECES, 2 * TILE, PIECE), BF16),
                pltpu.VMEM((TILES, PIECES, 2 * TILE, PIECE), F32),
                pltpu.VMEM((TILES, KV_LOCAL, GROUP * TILE, 2 * HD), F32),
                pltpu.VMEM(stats, F32),
                pltpu.VMEM(stats, F32),
                pltpu.VMEM(stats, F32),
                pltpu.VMEM((ROWS, WIDE), BF16),
                pltpu.VMEM((ROWS, WIDE), BF16),
                dma((4,)),
                dma((2,)),
                dma((2,)),
                dma((2,)),
                dma((2,)),
                dma((MOST,)),
                dma((SLOTS - 1, CHUNKS)),
                dma((TILES, KV_LOCAL)),
                dma((TILES, KV_LOCAL)),
                dma((TILES, PIECES)),
                dma((TILES, PIECES)),
                dma((TILES, PIECES, 2)),
            ],
            compiler_params=pltpu.CompilerParams(
                collective_id=0, has_side_effects=True, vmem_limit_bytes=56 << 20
            ),
            cost_estimate=pl.CostEstimate(
                flops=8 << 30, bytes_accessed=14 << 20, transcendentals=1 << 21
            ),
            name="tangent_layer",
        )(q, *(a.reshape(CHUNKS, PART, 2 * HD) for a in (k, v)), qt,
          *(a.reshape(CHUNKS, PART, 2 * HD) for a in (kt, vt)), seg.reshape(1, ROWS), w)
        return pl.pallas_call(
            copy_kernel,
            out_shape=results,
            in_specs=[anywhere, anywhere],
            out_specs=[anywhere, anywhere],
            scratch_shapes=[
                pltpu.VMEM((ROWS, WIDE), BF16),
                pltpu.VMEM((ROWS, WIDE), BF16),
                dma((HANDS, 2)),
                dma((HANDS, 2)),
            ],
            cost_estimate=pl.CostEstimate(flops=0, bytes_accessed=2 << 20, transcendentals=0),
            name="hand_over",
        )(*outs)

    return jax.shard_map(
        per_device,
        mesh=mesh,
        in_specs=(
            P("seq", "head"),
            P("seq", "head"),
            P("seq", "head"),
            P("seq", "head"),
            P("seq", "head"),
            P("seq", "head"),
            P("seq"),
            P("head", None),
        ),
        out_specs=(P("seq", "head"), P("seq", "head")),
        check_vma=False,
    )
```

time: 245 us -> 58 us (0.24); the launches traced: 241 us -> 57.8 us
  waiting for transfers between devices: 107 us -> 0 us
  Pallas kernels: 0 us -> 57 us
  starting transfers between devices: 52.4 us -> 0 us
  matrix products: 43.6 us -> 0 us
  between operations: 16.9 us -> 0.8 us
  local copies, waits for them, and re-layouts: 12.8 us -> 0 us
  other arithmetic: 7.37 us -> 0 us
    reduce_scatter x2 -> x0, waiting for transfers between devices: 104 us -> none  [the longest x1 68.5 us: per_device(): lax.psum_scatter(out_term.astype(jnp.bfloat16), 'head', scatter_dimension...]
    pallas_call x0 -> x2, Pallas kernels: none -> 57 us  [the longest x1 55 us: per_device(): pl.pallas_call(functools.partial(kernel, n_seq), out_shape=results, in_sp...]
    ppermute x15 -> x0, starting transfers between devices: 52.3 us -> none  [passed_along(): lax.ppermute(value, axis, [(source, source + steps) for source in range(l...]
    dot_general x14 -> x0, matrix products: 43.6 us -> none  [the longest x2 7.4 us: score_pair(): jnp.einsum('qhgd,khd->qhgk', q_heads, kt_heads, preferred_element_type=jn...]
    reshape x8 -> x0, local copies, waits for them, and re-layouts: 5.83 us -> none  [key_view(): return block.reshape(block.shape[0], block.shape[1] // HD, HD)]
    cond x19 -> x0, local copies, waits for them, and re-layouts: 4.48 us -> none  [the longest x2 2.89 us: fold_block(): return lax.cond(jnp.any(allowed), update, keep_same, carry)]
    ppermute x15 -> x0, waiting for transfers between devices: 3.88 us -> none  [passed_along(): lax.ppermute(value, axis, [(source, source + steps) for source in range(l...]
    unnamed x12 -> x0, local copies, waits for them, and re-layouts: 2.52 us -> none
  transfers between devices with their start and end apart: 17 -> 0, of which waited for: 3 -> 0; matrix products, arithmetic and copies ran while one was open for 21% -> 0% of each run, Pallas kernels for 0% -> 0%
where the time goes in v1:
time: 58 us; the launch traced here: 57.8 us
  Pallas kernels  57 us (98%)
  between operations  0.8 us (1%)
    pallas_call x1, Pallas kernels, per_device(): pl.pallas_call(functools.partial(kernel, n_seq), out_shape=results, in_sp...  55 us
    pallas_call x1, Pallas kernels, per_device(): pl.pallas_call(copy_kernel, out_shape=results, in_specs=[anywhere, anywhe...  1.98 us

profile of v1, /device:TPU:112, one launch (start us, length us, event | category | flops | bytes accessed | tf_op | source)
XLA Modules:
  0.0 57.8 jit_solution(12509302203778353287)
XLA Ops:
  0.6 55.0 %tangent_layer.1 = (bf16[256,1024]{1,0:T(8,128)(2,1)}, bf16[256,1024]{1,0:T(8,128)(2,1)}) custom-call(bf16[256,1024]{1,0:T(8,128)(2,1)} %q_hbm.1, bf16[8,32,256]{2,1,0:T(8,128)(2,1)} %bitcast.5, bf16[8,32,256]{2,1,0:T(8,128)(2,1)} %bitcast.6, bf16[256,1024]{1,0:T(8,128)(2,1)} %qt_hbm.1, bf16[8,32,256]{2,1,0:T(8,128)(2,1)} %bitcast.7, ...), custom_call_target="tpu_custom_call" | custom-call | flops 8589934592 | bytes 14680064 | tf_op jit(solution)/shard_map/tangent_layer/pallas_call | solution.py:609
  55.7 2.0 %hand_over.1 = (bf16[256,1024]{1,0:T(8,128)(2,1)}, bf16[256,1024]{1,0:T(8,128)(2,1)}) custom-call(bf16[256,1024]{1,0:T(8,128)(2,1)} %get-tuple-element.4.a_hbm, bf16[256,1024]{1,0:T(8,128)(2,1)} %get-tuple-element.5.b_hbm), custom_call_target="tpu_custom_call" | custom-call | bytes 2097152 | tf_op jit(solution)/shard_map/hand_over/pallas_call | solution.py:651
